TPU v7x, 128 devices: a whole 4x4x4 slice. The times are simulated.
128 devices in a mesh: box: 8 (over y, core), ctr: 16 (over z, x).
Axes of the slice: x: 4, y: 4, z: 4, core: 2. Of those that a mesh axis runs over, the one named last changes fastest.
Arguments:
- box_locals: bfloat16 [289, 16384], P(None, 'box'), may hold values from -6 to 6
- centre_box: int32 [262144], P(('box', 'ctr')), may hold values from 0 to 16383, as said below
- centre_rho: float32 [262144], P(('box', 'ctr')), may hold values from 0.85 to 1
- panel_sources: bfloat16 [131072, 128], P('ctr'), may hold values from -6 to 6
- centre_near: int32 [8, 262144], P(None, ('box', 'ctr')), may hold values from 0 to 131071, as said below
- near_count: int32 [262144], P(('box', 'ctr')), may hold values from 1 to 8
- l2l_op: bfloat16 [289, 289], replicated, may hold values from -0.375 to 0.375
- p2l_op: bfloat16 [289, 128], replicated, may hold values from -0.5 to 0.5
- target_coords: float32 [2, 4, 262144], P(None, None, ('box', 'ctr')), may hold values from -1 to 1
Outputs:
- potential: float32 [4, 262144], P(None, ('box', 'ctr'))
Inputs may be any that keep to these rules, and one draw needn't show every extreme that they name: `centre_box`: Non-decreasing over the centres of one index of box. The centres of box index b name boxes of shard b (boxes b * 2048 to (b + 1) * 2048 - 1) and, a few at its end, boxes among the first 2048 // 32 (at least one) of shard b + 1. `centre_near`: slots at or beyond a centre's near_count are to be ignored. For a centre of ctr index q, slots 0 to 6 name panels p with (p - q * 8192 + 8192 // 4) mod 131072 below 12288. Slot 7 of the i-th centre of a device at ctr index q names a panel of ctr index (q + 1 + (i + r) mod (15)) mod 16, with one r for each device. Roughly a seventh of the used slots name panels of another ctr index.
All inputs are finite; a program needn't handle non-finite values.
Results may differ from a plain program's by a relative error of at most 0.0028.
Values may be sent and summed in bfloat16 or wider, within the bound.
A program may use at most 128 MiB of HBM per device.

v0:
```python
import jax
import jax.numpy as jnp
from jax import lax
from jax.sharding import PartitionSpec as P

ORDER = 16


def from_behind(value, axis, steps):
    count = lax.axis_size(axis)
    first, last = (max(0, -steps), min(count, count - steps))
    return lax.ppermute(value, axis, [(source, source + steps) for source in range(first, last)])


def chebyshev(values, order):
    terms = [jnp.ones_like(values), values]
    for level in range(2, order + 1):
        terms.append(2.0 * values * terms[-1] - terms[-2])
    return jnp.stack(terms[: order + 1])


def degree_table(order):
    steps = jnp.arange(order + 1, dtype=jnp.float32)
    return (steps[:, None] + steps[None, :]).reshape(-1)


def shards(
    box_locals,
    centre_box,
    centre_rho,
    panel_sources,
    centre_near,
    near_count,
    l2l_op,
    p2l_op,
    target_coords,
):
    ctr_local = centre_box.shape[0]
    box_width = box_locals.shape[1]
    next_shard = from_behind(box_locals, "box", -1)
    joined = jnp.concatenate([box_locals, next_shard], axis=1)
    box_offset = centre_box - lax.axis_index("box") * box_width
    column_ids = jnp.arange(2 * box_width, dtype=jnp.int32)
    picker = (column_ids[:, None] == box_offset[None, :]).astype(jnp.bfloat16)
    box_picked = jnp.dot(joined, picker, preferred_element_type=jnp.float32).astype(jnp.bfloat16)
    all_panels = lax.all_gather(panel_sources, "ctr", axis=0, tiled=True)
    near_sum = jnp.zeros((ctr_local, panel_sources.shape[1]), jnp.float32)
    for slot in range(centre_near.shape[0]):
        rows = jnp.take(all_panels, centre_near[slot], axis=0).astype(jnp.float32)
        near_sum = near_sum + jnp.where((slot < near_count)[:, None], rows, 0.0)
    near_round = near_sum.astype(jnp.bfloat16)
    scale = jnp.exp(degree_table(ORDER)[:, None] * jnp.log(centre_rho)[None, :])
    translated = jnp.dot(l2l_op, box_picked, preferred_element_type=jnp.float32)
    direct = jnp.einsum("ks,cs->kc", p2l_op, near_round, preferred_element_type=jnp.float32)
    centre_exp = scale * translated + direct
    grid = centre_exp.reshape(ORDER + 1, ORDER + 1, -1)
    cheb_u = chebyshev(target_coords[0], ORDER)
    cheb_v = chebyshev(target_coords[1], ORDER)
    return jnp.einsum("ijc,itc,jtc->tc", grid, cheb_u, cheb_v, precision=lax.Precision.HIGHEST)


def solution(mesh):
    in_specs = (
        P(None, "box"),
        P(("box", "ctr")),
        P(("box", "ctr")),
        P("ctr", None),
        P(None, ("box", "ctr")),
        P(("box", "ctr")),
        P(),
        P(),
        P(None, None, ("box", "ctr")),
    )
    out_specs = P(None, ("box", "ctr"))
    return jax.shard_map(shards, mesh=mesh, in_specs=in_specs, out_specs=out_specs, check_vma=False)
```

profile of v0, /device:TPU:0, one launch (start us, length us, event | category | flops | bytes accessed | tf_op | source)
XLA Modules:
  0.0 522.2 jit_solution(16422303363387610190)
XLA Ops:
  6.5 0.7 all-gather.2.cloned.1.call-update
  7.3 1.3 collective-permute-start
  10.0 1.3 fusion.50
  11.3 0.8 constant_dynamic-update-slice_fusion.15
  12.1 0.8 constant_dynamic-update-slice_fusion.14
  12.9 0.8 constant_dynamic-update-slice_fusion.13
  13.7 0.8 constant_dynamic-update-slice_fusion.12
  14.5 0.8 constant_dynamic-update-slice_fusion.11
  15.2 0.8 constant_dynamic-update-slice_fusion.10
  16.0 0.8 constant_dynamic-update-slice_fusion.9
  16.8 0.8 constant_dynamic-update-slice_fusion.8
  17.6 0.8 constant_dynamic-update-slice_fusion.7
  18.5 0.8 constant_dynamic-update-slice_fusion.6
  19.3 0.8 constant_dynamic-update-slice_fusion.5
  20.1 0.8 constant_dynamic-update-slice_fusion.4
  21.7 3.2 copy.10
  25.0 10.1 %fusion.3 = f32[289,2048]{1,0:T(8,128)} fusion(bf16[289,289]{1,0:T(8,128)(2,1)S(1)} %copy-done, s32[2048]{0:T(1024)S(1)} %broadcast_subtract_fusion, bf16[289,2048]{1,0:T(8,128)(2,1)} %collective-permute-done, bf16[289,2048]{1,0:T(8,128)(2,1)S(1)} %copy-done.4, f32[2048]{0:T(1024)S(1)} %log.3, f32[289]{0:T(512)S(1)} %add.85), kind=kOutput, calls=%fused_computation.14 | convolution fusion | flops 5205616640 | bytes 4919558 | tf_op jit(solution)/shard_map/dot_general | solution.py:53
  35.0 174.2 %all-gather.2.cloned.1.call-done = bf16[131072,128]{1,0:T(8,128)(2,1)} async-done(((bf16[8192,128]{1,0:T(8,128)(2,1)}), bf16[131072,128]{1,0:T(8,128)(2,1)}) %all-gather.2.cloned.1.call-update) | async-done | bytes 33554448 | tf_op jit(solution)/shard_map/all_gather | solution.py:46
  209.2 30.9 %gather_fusion.6 = bf16[2048,128]{1,0:T(8,128)(2,1)} fusion(bf16[131072,128]{1,0:T(8,128)(2,1)} %all-gather.2.cloned.1.call-done, s32[2048]{0:T(1024)S(1)} %get-tuple-element.50), kind=kCustom, calls=%fused_computation.6.clone | custom fusion | bytes 1056768 | tf_op jit(solution)/shard_map/jit(_take)/gather | solution.py:49
  240.2 30.9 %gather_fusion.2 = bf16[2048,128]{1,0:T(8,128)(2,1)} fusion(bf16[131072,128]{1,0:T(8,128)(2,1)} %all-gather.2.cloned.1.call-done, s32[2048]{0:T(1024)S(1)} %get-tuple-element.46), kind=kCustom, calls=%fused_computation.2.clone | custom fusion | bytes 1056768 | tf_op jit(solution)/shard_map/jit(_take)/gather | solution.py:49
  271.1 31.0 %gather_fusion = bf16[2048,128]{1,0:T(8,128)(2,1)} fusion(bf16[131072,128]{1,0:T(8,128)(2,1)} %all-gather.2.cloned.1.call-done, s32[2048]{0:T(1024)S(1)} %get-tuple-element.44), kind=kCustom, calls=%fused_computation.clone | custom fusion | bytes 1056768 | tf_op jit(solution)/shard_map/jit(_take)/gather | solution.py:49
  302.0 30.9 %gather_fusion.4 = bf16[2048,128]{1,0:T(8,128)(2,1)} fusion(bf16[131072,128]{1,0:T(8,128)(2,1)} %all-gather.2.cloned.1.call-done, s32[2048]{0:T(1024)S(1)} %get-tuple-element.48), kind=kCustom, calls=%fused_computation.4.clone | custom fusion | bytes 1056768 | tf_op jit(solution)/shard_map/jit(_take)/gather | solution.py:49
  333.0 30.9 %gather_fusion.7 = bf16[2048,128]{1,0:T(8,128)(2,1)} fusion(bf16[131072,128]{1,0:T(8,128)(2,1)} %all-gather.2.cloned.1.call-done, s32[2048]{0:T(1024)S(1)} %get-tuple-element.51), kind=kCustom, calls=%fused_computation.7.clone | custom fusion | bytes 1056768 | tf_op jit(solution)/shard_map/jit(_take)/gather | solution.py:49
  363.9 30.9 %gather_fusion.3 = bf16[2048,128]{1,0:T(8,128)(2,1)} fusion(bf16[131072,128]{1,0:T(8,128)(2,1)} %all-gather.2.cloned.1.call-done, s32[2048]{0:T(1024)S(1)} %get-tuple-element.47), kind=kCustom, calls=%fused_computation.3.clone | custom fusion | bytes 1056768 | tf_op jit(solution)/shard_map/jit(_take)/gather | solution.py:49
  394.8 30.9 %gather_fusion.1 = bf16[2048,128]{1,0:T(8,128)(2,1)} fusion(bf16[131072,128]{1,0:T(8,128)(2,1)} %all-gather.2.cloned.1.call-done, s32[2048]{0:T(1024)S(1)} %get-tuple-element.45), kind=kCustom, calls=%fused_computation.1.clone | custom fusion | bytes 1056768 | tf_op jit(solution)/shard_map/jit(_take)/gather | solution.py:49
  425.7 30.9 %gather_fusion.5 = bf16[2048,128]{1,0:T(8,128)(2,1)} fusion(bf16[131072,128]{1,0:T(8,128)(2,1)} %all-gather.2.cloned.1.call-done, s32[2048]{0:T(1024)S(1)} %get-tuple-element.49), kind=kCustom, calls=%fused_computation.5.clone | custom fusion | bytes 1056768 | tf_op jit(solution)/shard_map/jit(_take)/gather | solution.py:49
  456.6 9.1 %fusion.2 = f32[289,2048]{1,0:T(8,128)S(1)} fusion(f32[289,2048]{1,0:T(8,128)} %fusion.3, bf16[289,128]{1,0:T(8,128)(2,1)S(1)} %copy-done.5, bf16[2048,128]{1,0:T(8,128)(2,1)} %gather_fusion.7, bf16[2048,128]{1,0:T(8,128)(2,1)} %gather_fusion.6, bf16[2048,128]{1,0:T(8,128)(2,1)} %gather_fusion.5, bf16[2048,128]{1,0:T(8,128)(2,1)} %gather_fusion.4, ...), kind=kOutput, calls=%fused_computation.12 | convolution fusion | flops 160499712 | bytes 9036032 | tf_op jit(solution)/shard_map/ks,cs->kc/dot_general | solution.py:54
  465.7 2.1 reshape.32
  467.8 15.1 %copy.11 = f32[17,17,2048]{1,0,2:T(8,128)} copy(f32[17,17,2048]{2,1,0:T(8,128)} %reshape.32) | data formatting | bytes 4734976 | tf_op jit(solution)/shard_map/reshape | solution.py:56
  482.8 28.1 %fusion.51 = f32[2048,4,17]{2,1,0:T(4,128)} fusion(f32[17,4,2048]{0,1,2:T(4,128)} %copy.10, f32[17,17,2048]{1,0,2:T(8,128)} %copy.11), kind=kOutput, calls=%fused_computation.148 | convolution fusion | flops 28409856 | bytes 3481600 | tf_op jit(solution)/shard_map/ijc,itc,jtc->tc/dot_general | solution.py:59
  511.0 3.6 copy.12
  514.5 0.8 fusion.11
  (45 shorter events, 2.3 us)
Async XLA Ops:
  6.5 18.4 %copy-start = (bf16[289,289]{1,0:T(8,128)(2,1)S(1)}, bf16[289,289]{1,0:T(8,128)(2,1)}, u32[]{:S(2)}) copy-start(bf16[289,289]{1,0:T(8,128)(2,1)} %param.17) | copy-start | bytes 501130
  6.5 14.3 %copy-start.2 = (f32[2,4,2048]{2,1,0:T(4,128)S(1)}, f32[2,4,2048]{2,1,0:T(4,128)}, u32[]{:S(2)}) copy-start(f32[2,4,2048]{2,1,0:T(4,128)} %param.19) | copy-start | bytes 196612
  6.5 202.7 %all-gather.2.cloned.1.call-start = ((), (), s32[]{:S(2)}) async-start(), calls=%async_computation | async-start | bytes 35651584 | tf_op jit(solution)/shard_map/all_gather | solution.py:46
  7.3 17.7 %collective-permute-start = (bf16[289,2048]{1,0:T(8,128)(2,1)}, bf16[289,2048]{1,0:T(8,128)(2,1)}, u32[]{:S(2)}, u32[]{:S(2)}) collective-permute-start(bf16[289,2048]{1,0:T(8,128)(2,1)} %param.11), channel_id=1, source_target_pairs={{16,0},{32,16},{48,32},{64,48},{80,64},{96,80},{112,96},{17,1},{33... | collective-permute-start | bytes 3551240 | tf_op jit(solution)/shard_map/ppermute | solution.py:12
  21.0 3.9 copy-start.3
  21.0 4.0 copy-start.4
  425.7 30.9 %copy-start.5 = (bf16[289,128]{1,0:T(8,128)(2,1)S(1)}, bf16[289,128]{1,0:T(8,128)(2,1)}, u32[]{:S(2)}) copy-start(bf16[289,128]{1,0:T(8,128)(2,1)} %param.18) | copy-start | bytes 221956
  482.8 32.5 %copy-start.1 = (bf16[289,289]{1,0:T(8,128)(2,1)S(1)}, bf16[289,289]{1,0:T(8,128)(2,1)}, u32[]{:S(2)}) copy-start(bf16[289,289]{1,0:T(8,128)(2,1)} %param.17) | copy-start | bytes 501130
Sparse Core Ops, SparseCore 0:
  9.5 199.6 all-gather.1
where the time goes:
time: 526 us; the launch traced here: 522 us
  local copies, waits for them, and re-layouts  274 us (52%)
  waiting for transfers between devices  175 us (33%)
  matrix products  47.3 us (9%)
  between operations  13.6 us (3%)
  other arithmetic  11 us (2%)
    gather x8, local copies, waits for them, and re-layouts, shards(): rows = jnp.take(all_panels, centre_near[slot], axis=0).astype(jnp.float32)  247 us
    all_gather x1, waiting for transfers between devices, shards(): all_panels = lax.all_gather(panel_sources, 'ctr', axis=0, tiled=True)  174 us
    dot_general x1, matrix products, shards(): jnp.einsum('ijc,itc,jtc->tc', grid, cheb_u, cheb_v, precision=lax.Precisi...  28.1 us
    reshape x2, local copies, waits for them, and re-layouts, shards(): grid = centre_exp.reshape(ORDER + 1, ORDER + 1, -1)  17.1 us
  transfers between devices with their start and end apart: 2, of which 1 were waited for; matrix products, arithmetic and copies ran while one was open for 5% of the time, Pallas kernels for 0%

commit v1 on v0

v1 whole, which is shorter than its diff:
```python
import functools

import jax
import jax.numpy as jnp
from jax import lax
from jax.experimental import pallas as pl
from jax.experimental.pallas import tpu as pltpu
from jax.sharding import PartitionSpec as P

N_CTR = 16
N_BOX = 8
CTR = 2048
PAN = 8192
MARGIN = 2048
COEF = 289
DEG = 17
SRC = 128
BOXES = 2048
KP = 296
ZERO_ROW = PAN + 2 * MARGIN
TAB = ZERO_ROW + 8
RING = N_CTR - 1
REQ = 2176
FAR = 144
FAR_USED = 137
HALF = MARGIN // 2
BLOCK = 256
UNROLL = 32
MESH = pl.DeviceIdType.MESH
F32 = jnp.float32
BF16 = jnp.bfloat16


def evaluate(grid, table, tile):
    out = []
    for t in range(4):
        acc = None
        for b in range(DEG):
            term = grid[16 * b:16 * b + 16, :] * table[tile, pl.ds(8 * b + 4 + t, 1), :]
            acc = term if acc is None else acc + term
        acc = acc * table[tile, pl.ds(t, 16, stride=8), :]
        last = grid[272:296, :] * table[tile, pl.ds(4 + t, 24, stride=8), :]
        last = last * table[tile, pl.ds(8 * 16 + t, 1), :]
        total = (acc[0:8] + acc[8:16]) + (last[0:8] + last[8:16] + last[16:24])
        out.append(jnp.sum(total, axis=0, keepdims=True))
    return jnp.concatenate(out, axis=0)


def fill(table, xy_ref, rho_ref):
    def one(tile, _):
        lanes = pl.ds(pl.multiple_of(tile * 128, 128), 128)
        x = xy_ref[:, lanes]
        square = None
        if rho_ref is not None:
            rho = rho_ref[:, lanes]
            x, square = x * rho, rho * rho
        before, now = jnp.ones_like(x), x
        table[tile, pl.ds(0, 8), :] = before
        table[tile, pl.ds(8, 8), :] = now
        for n in range(2, DEG):
            later = 2.0 * x * now - (before if square is None else square * before)
            table[tile, pl.ds(8 * n, 8), :] = later
            before, now = now, later
        table[tile, pl.ds(8 * DEG, 56), :] = jnp.zeros((56, 128), F32)
        return 0

    lax.fori_loop(0, CTR // 128, one, 0)


def kernel(
    box_hbm, cbox_ref, rho_ref, pan_hbm, near_ref, count_ref, l2l_ref, p2l_ref, xy_ref,
    out_ref,
    loc, boxv, boxn, prevb, nextb, tab, idx_v, req_v, reqs_v, stage, send_v, far, acc, tplain, tscaled, l2, p2, potb,
    idx_s, req_s,
    loc_sem, margin_send, margin_recv, share_send, share_recv, box_sems, req_send, req_recv, far_send, far_recv, smem_sems,
):
    b, q = lax.axis_index("box"), lax.axis_index("ctr")
    core = lax.rem(b, 2)
    sibling = b + 1 - 2 * core

    def on_ctr(other):
        return (b, other)

    load_pan = pltpu.make_async_copy(pan_hbm, loc, loc_sem.at[0])
    load_box = pltpu.make_async_copy(box_hbm, boxv, loc_sem.at[1])
    load_pan.start()
    load_box.start()

    barrier = pltpu.get_barrier_semaphore()

    def greet(o, _):
        pl.semaphore_signal(barrier, inc=1, device_id=on_ctr(lax.rem(q + o, N_CTR)), device_id_type=MESH)
        return 0

    lax.fori_loop(1, N_CTR, greet, 0)
    for step in (1, N_BOX - 1):
        pl.semaphore_signal(barrier, inc=1, device_id=(lax.rem(b + step, N_BOX), q), device_id_type=MESH)

    slot7 = near_ref[7:8, :]
    count = count_ref[...]
    i = lax.broadcasted_iota(jnp.int32, (1, CTR), 1)
    rem15 = i - 15 * ((i * 34953) >> 19)
    shift = (((slot7 >> 13) - q) & 15) - 1 - rem15
    shift = jnp.where(shift < 0, shift + 15, shift)
    full = count == 8
    r = jnp.clip(jnp.max(jnp.where(full, shift, 0)), 0, 14)
    req_v[0:1, 0:CTR] = jnp.where(full, (slot7 & (PAN - 1)) + MARGIN, ZERO_ROW)
    lane = lax.broadcasted_iota(jnp.int32, (1, REQ - CTR), 1)
    req_v[0:1, CTR:REQ] = jnp.where(lane == REQ - CTR - 1, r, ZERO_ROW)
    near = near_ref[...]
    slot = lax.broadcasted_iota(jnp.int32, (8, CTR), 0)
    idx_v[...] = jnp.where(slot < count, (near - q * PAN + MARGIN) & (N_CTR * PAN - 1), ZERO_ROW)

    pl.semaphore_wait(barrier, RING + 2)

    right, left = lax.rem(q + 1, N_CTR), lax.rem(q + RING, N_CTR)
    my_half = pl.ds(pl.multiple_of(core * HALF, HALF), HALF)
    to_right = pltpu.make_async_remote_copy(
        pan_hbm.at[pl.ds(pl.multiple_of(PAN - MARGIN + core * HALF, HALF), HALF), :], prevb.at[my_half, :],
        margin_send.at[0], margin_recv.at[0], device_id=on_ctr(right), device_id_type=MESH)
    to_left = pltpu.make_async_remote_copy(
        pan_hbm.at[my_half, :], nextb.at[my_half, :],
        margin_send.at[1], margin_recv.at[1], device_id=on_ctr(left), device_id_type=MESH)
    to_right.start()
    to_left.start()
    box_copy = pltpu.make_async_remote_copy(
        box_hbm.at[:, pl.ds(0, 128)], boxn, box_sems.at[0], box_sems.at[1],
        device_id=(lax.rem(b + N_BOX - 1, N_BOX), q), device_id_type=MESH)
    box_copy.start()

    def request(o):
        return pltpu.make_async_remote_copy(
            req_v, reqs_v.at[o - 1], req_send.at[o - 1], req_recv.at[o - 1],
            device_id=on_ctr(lax.rem(q + o, N_CTR)), device_id_type=MESH)

    def ask(o, _):
        request(o).start()
        return 0

    lax.fori_loop(1, N_CTR, ask, 0)

    for j in range(7):
        pltpu.make_async_copy(idx_v.at[j], idx_s.at[pl.ds(j * CTR, CTR)], smem_sems.at[RING + j]).start()

    tab[pl.ds(ZERO_ROW, 8), :] = jnp.zeros((8, SRC), F32)
    load_pan.wait()

    def widen(k, _):
        rows = pl.ds(pl.multiple_of(k * 512, 512), 512)
        tab[pl.ds(pl.multiple_of(MARGIN + k * 512, 512), 512), :] = loc[rows, :].astype(F32)
        return 0

    lax.fori_loop(0, PAN // 512, widen, 0)

    fill(tplain, xy_ref, None)
    fill(tscaled, xy_ref, rho_ref)

    row = lax.broadcasted_iota(jnp.int32, (KP, COEF), 0)
    col = lax.broadcasted_iota(jnp.int32, (KP, COEF), 1)
    source = jnp.where(row < 272, (row & 15) * DEG + (row >> 4), 16 * DEG + row - 272)
    order = (col == source).astype(F32).astype(BF16)
    l2[...] = jnp.dot(order, l2l_ref[...], preferred_element_type=F32).astype(BF16)
    p2[...] = jnp.dot(order, p2l_ref[...], preferred_element_type=F32).astype(BF16)

    def take_request(o, _):
        request(o).wait_recv()
        pltpu.make_async_copy(reqs_v.at[o - 1, 0], req_s.at[pl.ds((o - 1) * REQ, REQ)], smem_sems.at[o - 1]).start()
        return 0

    lax.fori_loop(1, N_CTR, take_request, 0)

    def answer(o):
        return pltpu.make_async_remote_copy(
            send_v.at[o - 1], far.at[o - 1], far_send.at[o - 1], far_recv.at[o - 1],
            device_id=on_ctr(lax.rem(q + N_CTR - o, N_CTR)), device_id_type=MESH)

    def have_request(o, _):
        pltpu.make_async_copy(reqs_v.at[o - 1, 0], req_s.at[pl.ds((o - 1) * REQ, REQ)], smem_sems.at[o - 1]).wait()
        return 0

    lax.fori_loop(1, N_CTR, have_request, 0)

    def serve(o, _):
        base = (o - 1) * REQ
        shift = req_s[base + REQ - 1]
        first = lax.rem(o + 14 - shift, RING)
        mine = req_s.at[pl.ds(base + first, 15 * (FAR_USED - 1) + 1)]
        for k in range(FAR_USED):
            stage[pl.ds(k, 1), :] = tab[pl.ds(mine[15 * k], 1), :]
        send_v[o - 1] = stage[...].astype(BF16)
        answer(o).start()
        return 0

    stage[pl.ds(FAR - 8, 8), :] = jnp.zeros((8, SRC), F32)
    lax.fori_loop(1, N_CTR, serve, 0)

    def share(k, buffer):
        return pltpu.make_async_remote_copy(
            buffer.at[my_half, :], buffer.at[my_half, :], share_send.at[k], share_recv.at[k],
            device_id=(sibling, q), device_id_type=MESH)

    to_right.wait_recv()
    share(0, prevb).start()
    to_left.wait_recv()
    share(1, nextb).start()

    load_box.wait()
    box_copy.wait_recv()

    def box_block(k, _):
        lanes = pl.ds(pl.multiple_of(k * BLOCK, BLOCK), BLOCK)
        offset = cbox_ref[:, lanes] - b * BOXES
        ids = lax.broadcasted_iota(jnp.int32, (BOXES, BLOCK), 0)
        picked = jnp.dot(boxv[...], (ids == offset).astype(F32).astype(BF16), preferred_element_type=F32)
        ids = lax.broadcasted_iota(jnp.int32, (128, BLOCK), 0) + BOXES
        picked += jnp.dot(boxn[...], (ids == offset).astype(F32).astype(BF16), preferred_element_type=F32)
        moved = jnp.dot(l2[...], picked.astype(BF16), preferred_element_type=F32)
        for h in range(BLOCK // 128):
            part = evaluate(moved[:, 128 * h:128 * h + 128], tscaled, k * (BLOCK // 128) + h)
            potb[:, pl.ds(pl.multiple_of(k * BLOCK + 128 * h, 128), 128)] = part
        return 0

    lax.fori_loop(0, CTR // BLOCK, box_block, 0)

    share(0, prevb).wait_recv()
    share(1, nextb).wait_recv()

    def widen_margin(k, _):
        rows = pl.ds(pl.multiple_of(k * 512, 512), 512)
        tab[rows, :] = prevb[rows, :].astype(F32)
        tab[pl.ds(pl.multiple_of(MARGIN + PAN + k * 512, 512), 512), :] = nextb[rows, :].astype(F32)
        return 0

    lax.fori_loop(0, MARGIN // 512, widen_margin, 0)
    for j in range(7):
        pltpu.make_async_copy(idx_v.at[j], idx_s.at[pl.ds(j * CTR, CTR)], smem_sems.at[RING + j]).wait()

    def gather(k, _):
        c0 = k * UNROLL
        lists = [idx_s.at[pl.ds(j * CTR + c0, UNROLL)] for j in range(7)]
        for u in range(UNROLL):
            rows = [tab[pl.ds(lists[j][u], 1), :] for j in range(7)]
            while len(rows) > 1:
                rows = [x + y for x, y in zip(rows[::2], rows[1::2])] + ([rows[-1]] if len(rows) % 2 else [])
            acc[pl.ds(c0 + u, 1), :] = rows[0]
        return 0

    lax.fori_loop(0, CTR // UNROLL, gather, 0)

    def take_far(o, _):
        answer(o).wait_recv()
        return 0

    lax.fori_loop(1, N_CTR, take_far, 0)
    for m in range(RING):
        rows = far[lax.rem(m + r, RING)].astype(F32)
        at = pl.ds(m, FAR, stride=RING)
        acc[at, :] = acc[at, :] + rows

    def near_block(k, _):
        lanes = pl.ds(pl.multiple_of(k * BLOCK, BLOCK), BLOCK)
        near_round = acc[lanes, :].astype(BF16)
        direct = lax.dot_general(p2[...], near_round, (((1,), (1,)), ((), ())), preferred_element_type=F32)
        for h in range(BLOCK // 128):
            part = evaluate(direct[:, 128 * h:128 * h + 128], tplain, k * (BLOCK // 128) + h)
            cols = pl.ds(pl.multiple_of(k * BLOCK + 128 * h, 128), 128)
            out_ref[:, cols] = potb[:, cols] + part
        return 0

    lax.fori_loop(0, CTR // BLOCK, near_block, 0)

    to_right.wait_send()
    to_left.wait_send()
    box_copy.wait_send()
    share(0, prevb).wait_send()
    share(1, nextb).wait_send()

    def finish(o, _):
        request(o).wait_send()
        answer(o).wait_send()
        return 0

    lax.fori_loop(1, N_CTR, finish, 0)


def shards(box_locals, centre_box, centre_rho, panel_sources, centre_near, near_count, l2l_op, p2l_op, target_coords):
    vmem = pl.BlockSpec(memory_space=pltpu.VMEM)
    anywhere = pl.BlockSpec(memory_space=pl.ANY)
    dma = pltpu.SemaphoreType.DMA
    return pl.pallas_call(
        kernel,
        out_shape=jax.ShapeDtypeStruct((4, CTR), F32),
        in_specs=[anywhere, vmem, vmem, anywhere, vmem, vmem, vmem, vmem, vmem],
        out_specs=vmem,
        scratch_shapes=[
            pltpu.VMEM((PAN, SRC), BF16),
            pltpu.VMEM((COEF, BOXES), BF16),
            pltpu.VMEM((COEF, 128), BF16),
            pltpu.VMEM((MARGIN, SRC), BF16),
            pltpu.VMEM((MARGIN, SRC), BF16),
            pltpu.VMEM((TAB, SRC), F32),
            pltpu.VMEM((8, CTR), jnp.int32),
            pltpu.VMEM((1, REQ), jnp.int32),
            pltpu.VMEM((RING, 1, REQ), jnp.int32),
            pltpu.VMEM((FAR, SRC), F32),
            pltpu.VMEM((RING, FAR, SRC), BF16),
            pltpu.VMEM((RING, FAR, SRC), BF16),
            pltpu.VMEM((RING * FAR, SRC), F32),
            pltpu.VMEM((CTR // 128, 192, 128), F32),
            pltpu.VMEM((CTR // 128, 192, 128), F32),
            pltpu.VMEM((KP, COEF), BF16),
            pltpu.VMEM((KP, SRC), BF16),
            pltpu.VMEM((4, CTR), F32),
            pltpu.SMEM((7 * CTR,), jnp.int32),
            pltpu.SMEM((RING * REQ,), jnp.int32),
            dma((2,)), dma((2,)), dma((2,)), dma((2,)), dma((2,)), dma((2,)),
            dma((RING,)), dma((RING,)), dma((RING,)), dma((RING,)), dma((RING + 7,)),
        ],
        compiler_params=pltpu.CompilerParams(collective_id=0, has_side_effects=True, vmem_limit_bytes=60 * 2**20),
        name="qbx",
    )(
        box_locals, centre_box.reshape(1, CTR), centre_rho.reshape(1, CTR), panel_sources, centre_near,
        near_count.reshape(1, CTR), l2l_op, p2l_op, target_coords.reshape(8, CTR),
    )


def solution(mesh):
    in_specs = (
        P(None, "box"),
        P(("box", "ctr")),
        P(("box", "ctr")),
        P("ctr", None),
        P(None, ("box", "ctr")),
        P(("box", "ctr")),
        P(),
        P(),
        P(None, None, ("box", "ctr")),
    )
    out_specs = P(None, ("box", "ctr"))
    return jax.shard_map(shards, mesh=mesh, in_specs=in_specs, out_specs=out_specs, check_vma=False)
```

time: 526 us -> 44.9 us (0.09)
  local copies, waits for them, and re-layouts: 274 us -> 2.86 us
  waiting for transfers between devices: 175 us -> 0 us
  matrix products: 47.3 us -> 0 us
  Pallas kernels: 0 us -> 41.8 us
  between operations: 13.6 us -> 0.01 us
  other arithmetic: 11 us -> 0 us
    gather x8 -> x0, local copies, waits for them, and re-layouts: 247 us -> none  [shards(): rows = jnp.take(all_panels, centre_near[slot], axis=0).astype(jnp.float32)]
    all_gather x1 -> x0, waiting for transfers between devices: 174 us -> none  [shards(): all_panels = lax.all_gather(panel_sources, 'ctr', axis=0, tiled=True)]
    dot_general x3 -> x0, matrix products: 47.3 us -> none  [the longest x1 28.1 us: shards(): jnp.einsum('ijc,itc,jtc->tc', grid, cheb_u, cheb_v, precision=lax.Precisi...]
    pallas_call x0 -> x1, Pallas kernels: none -> 41.8 us  [shards(): pl.pallas_call(kernel, out_shape=jax.ShapeDtypeStruct((4, CTR), F32), in_...]
    reshape x2 -> x1, local copies, waits for them, and re-layouts: 17.1 us -> 1.48 us  [shards(): target_coords.reshape(8, CTR)]
    unnamed x26 -> x0, other arithmetic: 9.32 us -> none
  transfers between devices with their start and end apart: 2 -> 0, of which waited for: 1 -> 0; matrix products, arithmetic and copies ran while one was open for 5% -> 0% of each run, Pallas kernels for 0% -> 0%
where the time goes in v1:
time: 44.9 us; the launch traced here: 44.6 us
  Pallas kernels  41.8 us (93%)
  local copies, waits for them, and re-layouts  2.86 us (6%)
    pallas_call x1, Pallas kernels, shards(): pl.pallas_call(kernel, out_shape=jax.ShapeDtypeStruct((4, CTR), F32), in_...  41.8 us
    reshape x1, local copies, waits for them, and re-layouts, shards(): target_coords.reshape(8, CTR)  1.48 us
    unnamed x1, local copies, waits for them, and re-layouts  1.38 us

profile of v1, /device:TPU:0, one launch (start us, length us, event | category | flops | bytes accessed | tf_op | source)
XLA Modules:
  0.0 44.6 jit_solution(13243603032249597022)
XLA Ops:
  0.0 1.5 %reshape.15.xy_ref = f32[8,2048]{1,0:T(8,128)} reshape(f32[2,4,2048]{2,1,0:T(4,128)} %param.17) | data formatting | bytes 131072 | tf_op jit(solution)/shard_map/reshape | solution.py:323
  1.5 41.8 %qbx.1 = f32[4,2048]{1,0:T(4,128)} custom-call(bf16[289,2048]{1,0:T(8,128)(2,1)} %box_hbm.1, s32[1,2048]{1,0:T(1,128)} %bitcast.3, f32[1,2048]{1,0:T(1,128)} %bitcast.4, bf16[8192,128]{1,0:T(8,128)(2,1)} %pan_hbm.1, s32[8,2048]{1,0:T(8,128)} %near_ref.1, s32[1,2048]{1,0:T(1,128)} %bitcast.5, bf16[289,289]{1,0:T(8,128)(2,1)} %l2l_ref.1, ...), custom_call_target="tpu_custom_call" | custom-call | tf_op jit(solution)/shard_map/qbx/pallas_call | solution.py:290
  43.2 1.4 %copy.11 = f32[4,2048]{1,0:T(4,128)} copy(f32[4,2048]{1,0:T(4,128)} %qbx.1) | data formatting | bytes 65536

commit v2 on v1

--- a/solution.py
+++ b/solution.py
@@ -20,12 +20,13 @@
 ZERO_ROW = PAN + 2 * MARGIN
 TAB = ZERO_ROW + 8
 RING = N_CTR - 1
-REQ = 2176
+REQ = 256
 FAR = 144
 FAR_USED = 137
 HALF = MARGIN // 2
+FAR_ORDER = (5, 6, 7, 9, 10, 11, 13, 14, 15, 1, 2, 3, 4, 8, 12)
 BLOCK = 256
-UNROLL = 32
+UNROLL = 128
 MESH = pl.DeviceIdType.MESH
 F32 = jnp.float32
 BF16 = jnp.bfloat16
@@ -46,10 +47,10 @@
     return jnp.concatenate(out, axis=0)
 
 
-def fill(table, xy_ref, rho_ref):
+def fill(table, xy, rho_ref):
     def one(tile, _):
         lanes = pl.ds(pl.multiple_of(tile * 128, 128), 128)
-        x = xy_ref[:, lanes]
+        x = jnp.concatenate([xy[0, :, lanes], xy[1, :, lanes]], axis=0)
         square = None
         if rho_ref is not None:
             rho = rho_ref[:, lanes]
@@ -68,11 +69,12 @@
 
 
 def kernel(
-    box_hbm, cbox_ref, rho_ref, pan_hbm, near_ref, count_ref, l2l_ref, p2l_ref, xy_ref,
+    box_hbm, cbox_hbm, rho_hbm, pan_hbm, near_hbm, count_hbm, l2l_hbm, p2l_hbm, xy_hbm,
     out_ref,
-    loc, boxv, boxn, prevb, nextb, tab, idx_v, req_v, reqs_v, stage, send_v, far, acc, tplain, tscaled, l2, p2, potb,
+    boxv, cbox_ref, rho_ref, loc, near_ref, count_ref, l2l_ref, p2l_ref, xy_ref,
+    boxs, boxn, prevb, nextb, tab, idx_v, req_v, reqs_v, stage, send_v, far, acc, tplain, tscaled, l2, p2, potb,
     idx_s, req_s,
-    loc_sem, margin_send, margin_recv, share_send, share_recv, box_sems, req_send, req_recv, far_send, far_recv, smem_sems,
+    load_sems, margin_send, margin_recv, share_send, share_recv, box_sems, req_send, req_recv, far_send, far_recv, smem_sems,
 ):
     b, q = lax.axis_index("box"), lax.axis_index("ctr")
     core = lax.rem(b, 2)
@@ -81,12 +83,8 @@
     def on_ctr(other):
         return (b, other)
 
-    load_pan = pltpu.make_async_copy(pan_hbm, loc, loc_sem.at[0])
-    load_box = pltpu.make_async_copy(box_hbm, boxv, loc_sem.at[1])
-    load_pan.start()
-    load_box.start()
-
     barrier = pltpu.get_barrier_semaphore()
+
 
     def greet(o, _):
         pl.semaphore_signal(barrier, inc=1, device_id=on_ctr(lax.rem(q + o, N_CTR)), device_id_type=MESH)
@@ -96,6 +94,18 @@
     for step in (1, N_BOX - 1):
         pl.semaphore_signal(barrier, inc=1, device_id=(lax.rem(b + step, N_BOX), q), device_id_type=MESH)
 
+    loads = [
+        pltpu.make_async_copy(source, target, load_sems.at[k])
+        for k, (source, target) in enumerate([
+            (near_hbm, near_ref), (count_hbm, count_ref), (pan_hbm, loc), (xy_hbm, xy_ref), (rho_hbm, rho_ref),
+            (l2l_hbm, l2l_ref), (p2l_hbm, p2l_ref), (cbox_hbm, cbox_ref), (box_hbm, boxv),
+            (box_hbm.at[:, pl.ds(0, 128)], boxs)])
+    ]
+    for load in loads:
+        load.start()
+
+    loads[0].wait()
+    loads[1].wait()
     slot7 = near_ref[7:8, :]
     count = count_ref[...]
     i = lax.broadcasted_iota(jnp.int32, (1, CTR), 1)
@@ -104,46 +114,55 @@
     shift = jnp.where(shift < 0, shift + 15, shift)
     full = count == 8
     r = jnp.clip(jnp.max(jnp.where(full, shift, 0)), 0, 14)
-    req_v[0:1, 0:CTR] = jnp.where(full, (slot7 & (PAN - 1)) + MARGIN, ZERO_ROW)
-    lane = lax.broadcasted_iota(jnp.int32, (1, REQ - CTR), 1)
-    req_v[0:1, CTR:REQ] = jnp.where(lane == REQ - CTR - 1, r, ZERO_ROW)
-    near = near_ref[...]
+    below = jnp.where(full, ZERO_ROW - MARGIN - (slot7 & (PAN - 1)), 0)
+    turn = rem15 + r
+    turn = jnp.where(turn >= RING, turn - RING, turn)
+    mine = turn == lax.broadcasted_iota(jnp.int32, (16, CTR), 0)
+    high = jnp.where(mine, (below >> 7).astype(F32), 0.0)
+    low = jnp.where(mine, (below & 127).astype(F32), 0.0)
+    place = lax.broadcasted_iota(jnp.int32, (REQ, CTR), 0) == ((i * 34953) >> 19)
+    lists = lax.dot_general(
+        jnp.concatenate([high, low], axis=0).astype(BF16), place.astype(F32).astype(BF16),
+        (((1,), (1,)), ((), ())), preferred_element_type=F32).astype(jnp.int32)
+    lists = jnp.clip(ZERO_ROW - (lists[0:16] * 128 + lists[16:32]), 0, ZERO_ROW)
+    for o in range(1, N_CTR):
+        req_v[o - 1] = lists[o - 1:o]
     slot = lax.broadcasted_iota(jnp.int32, (8, CTR), 0)
-    idx_v[...] = jnp.where(slot < count, (near - q * PAN + MARGIN) & (N_CTR * PAN - 1), ZERO_ROW)
+    idx_v[...] = jnp.where(slot < count, (near_ref[...] - q * PAN + MARGIN) & (N_CTR * PAN - 1), ZERO_ROW)
+    to_smem = [pltpu.make_async_copy(idx_v.at[j], idx_s.at[pl.ds(j * CTR, CTR)], smem_sems.at[RING + j]) for j in range(7)]
+    for copy in to_smem:
+        copy.start()
 
     pl.semaphore_wait(barrier, RING + 2)
-
-    right, left = lax.rem(q + 1, N_CTR), lax.rem(q + RING, N_CTR)
-    my_half = pl.ds(pl.multiple_of(core * HALF, HALF), HALF)
-    to_right = pltpu.make_async_remote_copy(
-        pan_hbm.at[pl.ds(pl.multiple_of(PAN - MARGIN + core * HALF, HALF), HALF), :], prevb.at[my_half, :],
-        margin_send.at[0], margin_recv.at[0], device_id=on_ctr(right), device_id_type=MESH)
-    to_left = pltpu.make_async_remote_copy(
-        pan_hbm.at[my_half, :], nextb.at[my_half, :],
-        margin_send.at[1], margin_recv.at[1], device_id=on_ctr(left), device_id_type=MESH)
-    to_right.start()
-    to_left.start()
-    box_copy = pltpu.make_async_remote_copy(
-        box_hbm.at[:, pl.ds(0, 128)], boxn, box_sems.at[0], box_sems.at[1],
-        device_id=(lax.rem(b + N_BOX - 1, N_BOX), q), device_id_type=MESH)
-    box_copy.start()
 
     def request(o):
         return pltpu.make_async_remote_copy(
-            req_v, reqs_v.at[o - 1], req_send.at[o - 1], req_recv.at[o - 1],
+            req_v.at[o - 1], reqs_v.at[o - 1], req_send.at[o - 1], req_recv.at[o - 1],
             device_id=on_ctr(lax.rem(q + o, N_CTR)), device_id_type=MESH)
 
-    def ask(o, _):
+    for o in FAR_ORDER:
         request(o).start()
-        return 0
-
-    lax.fori_loop(1, N_CTR, ask, 0)
-
-    for j in range(7):
-        pltpu.make_async_copy(idx_v.at[j], idx_s.at[pl.ds(j * CTR, CTR)], smem_sems.at[RING + j]).start()
-
+
+    margins = []
+    for k, (buffer, step, start) in enumerate(((prevb, 1, PAN - MARGIN), (nextb, RING, 0))):
+        half = pl.ds(pl.multiple_of(core * HALF, HALF), HALF)
+        fetch = pltpu.make_async_remote_copy(
+            pan_hbm.at[pl.ds(pl.multiple_of(start + core * HALF, HALF), HALF), :], buffer.at[half, :],
+            margin_send.at[k], margin_recv.at[k], device_id=on_ctr(lax.rem(q + step, N_CTR)), device_id_type=MESH)
+        share = pltpu.make_async_remote_copy(
+            buffer.at[half, :], buffer.at[half, :], share_send.at[k], share_recv.at[k],
+            device_id=(sibling, q), device_id_type=MESH)
+        margins.append((fetch, share))
+    for fetch, _ in margins:
+        fetch.start()
+
+    box_copy = pltpu.make_async_remote_copy(
+        boxs, boxn, box_sems.at[0], box_sems.at[1],
+        device_id=(lax.rem(b + N_BOX - 1, N_BOX), q), device_id_type=MESH)
+    loads[9].wait()
+    box_copy.start()
     tab[pl.ds(ZERO_ROW, 8), :] = jnp.zeros((8, SRC), F32)
-    load_pan.wait()
+    loads[2].wait()
 
     def widen(k, _):
         rows = pl.ds(pl.multiple_of(k * 512, 512), 512)
@@ -151,10 +170,12 @@
         return 0
 
     lax.fori_loop(0, PAN // 512, widen, 0)
-
+    loads[3].wait()
+    loads[4].wait()
     fill(tplain, xy_ref, None)
     fill(tscaled, xy_ref, rho_ref)
-
+    loads[5].wait()
+    loads[6].wait()
     row = lax.broadcasted_iota(jnp.int32, (KP, COEF), 0)
     col = lax.broadcasted_iota(jnp.int32, (KP, COEF), 1)
     source = jnp.where(row < 272, (row & 15) * DEG + (row >> 4), 16 * DEG + row - 272)
@@ -162,49 +183,55 @@
     l2[...] = jnp.dot(order, l2l_ref[...], preferred_element_type=F32).astype(BF16)
     p2[...] = jnp.dot(order, p2l_ref[...], preferred_element_type=F32).astype(BF16)
 
+    def list_copy(o):
+        return pltpu.make_async_copy(reqs_v.at[o - 1, 0], req_s.at[pl.ds((o - 1) * REQ, REQ)], smem_sems.at[o - 1])
+
     def take_request(o, _):
         request(o).wait_recv()
-        pltpu.make_async_copy(reqs_v.at[o - 1, 0], req_s.at[pl.ds((o - 1) * REQ, REQ)], smem_sems.at[o - 1]).start()
+        list_copy(o).start()
         return 0
 
     lax.fori_loop(1, N_CTR, take_request, 0)
+
+    def have_request(o, _):
+        list_copy(o).wait()
+        return 0
+
+    lax.fori_loop(1, N_CTR, have_request, 0)
 
     def answer(o):
         return pltpu.make_async_remote_copy(
             send_v.at[o - 1], far.at[o - 1], far_send.at[o - 1], far_recv.at[o - 1],
             device_id=on_ctr(lax.rem(q + N_CTR - o, N_CTR)), device_id_type=MESH)
 
-    def have_request(o, _):
-        pltpu.make_async_copy(reqs_v.at[o - 1, 0], req_s.at[pl.ds((o - 1) * REQ, REQ)], smem_sems.at[o - 1]).wait()
-        return 0
-
-    lax.fori_loop(1, N_CTR, have_request, 0)
-
-    def serve(o, _):
+    def serve(k, _):
+        o = 4 * lax.rem(k // 3 + 1, 4) + 1 + lax.rem(k, 3)
+        serve_one(o)
+        return 0
+
+    def serve_column(k, _):
+        serve_one(4 * k)
+        return 0
+
+    def serve_one(o):
         base = (o - 1) * REQ
-        shift = req_s[base + REQ - 1]
-        first = lax.rem(o + 14 - shift, RING)
-        mine = req_s.at[pl.ds(base + first, 15 * (FAR_USED - 1) + 1)]
+        mine = req_s.at[pl.ds(base, FAR_USED)]
         for k in range(FAR_USED):
-            stage[pl.ds(k, 1), :] = tab[pl.ds(mine[15 * k], 1), :]
+            stage[pl.ds(k, 1), :] = tab[pl.ds(mine[k], 1), :]
         send_v[o - 1] = stage[...].astype(BF16)
+
+    stage[pl.ds(FAR - 8, 8), :] = jnp.zeros((8, SRC), F32)
+    lax.fori_loop(0, 12, serve, 0)
+    lax.fori_loop(1, 4, serve_column, 0)
+
+    for fetch, share in margins:
+        fetch.wait_recv()
+        share.start()
+    for o in FAR_ORDER:
         answer(o).start()
-        return 0
-
-    stage[pl.ds(FAR - 8, 8), :] = jnp.zeros((8, SRC), F32)
-    lax.fori_loop(1, N_CTR, serve, 0)
-
-    def share(k, buffer):
-        return pltpu.make_async_remote_copy(
-            buffer.at[my_half, :], buffer.at[my_half, :], share_send.at[k], share_recv.at[k],
-            device_id=(sibling, q), device_id_type=MESH)
-
-    to_right.wait_recv()
-    share(0, prevb).start()
-    to_left.wait_recv()
-    share(1, nextb).start()
-
-    load_box.wait()
+
+    loads[7].wait()
+    loads[8].wait()
     box_copy.wait_recv()
 
     def box_block(k, _):
@@ -222,8 +249,8 @@
 
     lax.fori_loop(0, CTR // BLOCK, box_block, 0)
 
-    share(0, prevb).wait_recv()
-    share(1, nextb).wait_recv()
+    for _, share in margins:
+        share.wait_recv()
 
     def widen_margin(k, _):
         rows = pl.ds(pl.multiple_of(k * 512, 512), 512)
@@ -232,8 +259,8 @@
         return 0
 
     lax.fori_loop(0, MARGIN // 512, widen_margin, 0)
-    for j in range(7):
-        pltpu.make_async_copy(idx_v.at[j], idx_s.at[pl.ds(j * CTR, CTR)], smem_sems.at[RING + j]).wait()
+    for copy in to_smem:
+        copy.wait()
 
     def gather(k, _):
         c0 = k * UNROLL
@@ -269,11 +296,10 @@
 
     lax.fori_loop(0, CTR // BLOCK, near_block, 0)
 
-    to_right.wait_send()
-    to_left.wait_send()
     box_copy.wait_send()
-    share(0, prevb).wait_send()
-    share(1, nextb).wait_send()
+    for group in margins:
+        for copy in group:
+            copy.wait_send()
 
     def finish(o, _):
         request(o).wait_send()
@@ -290,17 +316,25 @@
     return pl.pallas_call(
         kernel,
         out_shape=jax.ShapeDtypeStruct((4, CTR), F32),
-        in_specs=[anywhere, vmem, vmem, anywhere, vmem, vmem, vmem, vmem, vmem],
+        in_specs=[anywhere] * 9,
         out_specs=vmem,
         scratch_shapes=[
+            pltpu.VMEM((COEF, BOXES), BF16),
+            pltpu.VMEM((1, CTR), jnp.int32),
+            pltpu.VMEM((1, CTR), F32),
             pltpu.VMEM((PAN, SRC), BF16),
-            pltpu.VMEM((COEF, BOXES), BF16),
+            pltpu.VMEM((8, CTR), jnp.int32),
+            pltpu.VMEM((1, CTR), jnp.int32),
+            pltpu.VMEM((COEF, COEF), BF16),
+            pltpu.VMEM((COEF, SRC), BF16),
+            pltpu.VMEM((2, 4, CTR), F32),
+            pltpu.VMEM((COEF, 128), BF16),
             pltpu.VMEM((COEF, 128), BF16),
             pltpu.VMEM((MARGIN, SRC), BF16),
             pltpu.VMEM((MARGIN, SRC), BF16),
             pltpu.VMEM((TAB, SRC), F32),
             pltpu.VMEM((8, CTR), jnp.int32),
-            pltpu.VMEM((1, REQ), jnp.int32),
+            pltpu.VMEM((RING, 1, REQ), jnp.int32),
             pltpu.VMEM((RING, 1, REQ), jnp.int32),
             pltpu.VMEM((FAR, SRC), F32),
             pltpu.VMEM((RING, FAR, SRC), BF16),
@@ -313,14 +347,14 @@
             pltpu.VMEM((4, CTR), F32),
             pltpu.SMEM((7 * CTR,), jnp.int32),
             pltpu.SMEM((RING * REQ,), jnp.int32),
-            dma((2,)), dma((2,)), dma((2,)), dma((2,)), dma((2,)), dma((2,)),
+            dma((10,)), dma((2,)), dma((2,)), dma((2,)), dma((2,)), dma((2,)),
             dma((RING,)), dma((RING,)), dma((RING,)), dma((RING,)), dma((RING + 7,)),
         ],
         compiler_params=pltpu.CompilerParams(collective_id=0, has_side_effects=True, vmem_limit_bytes=60 * 2**20),
         name="qbx",
     )(
         box_locals, centre_box.reshape(1, CTR), centre_rho.reshape(1, CTR), panel_sources, centre_near,
-        near_count.reshape(1, CTR), l2l_op, p2l_op, target_coords.reshape(8, CTR),
+        near_count.reshape(1, CTR), l2l_op, p2l_op, target_coords,
     )
 
 

time: 44.9 us -> 36.4 us (0.81)
  Pallas kernels: 41.8 us -> 34.8 us
  local copies, waits for them, and re-layouts: 2.86 us -> 1.38 us
    pallas_call x1, Pallas kernels: 41.8 us -> 34.8 us  [shards(): pl.pallas_call(kernel, out_shape=jax.ShapeDtypeStruct((4, CTR), F32), in_...]
    reshape x1 -> x0, local copies, waits for them, and re-layouts: 1.48 us -> none  [shards(): target_coords.reshape(8, CTR)]
where the time goes in v2:
time: 36.4 us; the launch traced here: 36.2 us
  Pallas kernels  34.8 us (96%)
  local copies, waits for them, and re-layouts  1.38 us (4%)
    pallas_call x1, Pallas kernels, shards(): pl.pallas_call(kernel, out_shape=jax.ShapeDtypeStruct((4, CTR), F32), in_...  34.8 us
    unnamed x1, local copies, waits for them, and re-layouts  1.38 us

profile of v2, /device:TPU:0, one launch (start us, length us, event | category | flops | bytes accessed | tf_op | source)
XLA Modules:
  0.0 36.2 jit_solution(16668544700199682459)
XLA Ops:
  0.0 34.8 %qbx.1 = f32[4,2048]{1,0:T(4,128)} custom-call(bf16[289,2048]{1,0:T(8,128)(2,1)} %box_hbm.1, s32[1,2048]{1,0:T(1,128)} %bitcast.3, f32[1,2048]{1,0:T(1,128)} %bitcast.4, bf16[8192,128]{1,0:T(8,128)(2,1)} %pan_hbm.1, s32[8,2048]{1,0:T(8,128)} %near_hbm.1, s32[1,2048]{1,0:T(1,128)} %bitcast.5, bf16[289,289]{1,0:T(8,128)(2,1)} %l2l_hbm.1, ...), custom_call_target="tpu_custom_call" | custom-call | tf_op jit(solution)/shard_map/qbx/pallas_call | solution.py:316
  34.8 1.4 %copy.11 = f32[4,2048]{1,0:T(4,128)} copy(f32[4,2048]{1,0:T(4,128)} %qbx.1) | data formatting | bytes 65536

commit v3 on v2

--- a/solution.py
+++ b/solution.py
@@ -1,3 +1,5 @@
+import itertools
+
 import functools
 
 import jax
@@ -26,15 +28,20 @@
 HALF = MARGIN // 2
 FAR_ORDER = (5, 6, 7, 9, 10, 11, 13, 14, 15, 1, 2, 3, 4, 8, 12)
 BLOCK = 256
-UNROLL = 128
+BLOCKS = CTR // BLOCK
+PICKS = 4
+SPACING = 14
 MESH = pl.DeviceIdType.MESH
 F32 = jnp.float32
 BF16 = jnp.bfloat16
 
 
 def evaluate(grid, table, tile):
-    out = []
-    for t in range(4):
+    return jnp.concatenate([evaluate_one(grid, table, tile, t) for t in range(4)], axis=0)
+
+
+def evaluate_one(grid, table, tile, t):
+    if True:
         acc = None
         for b in range(DEG):
             term = grid[16 * b:16 * b + 16, :] * table[tile, pl.ds(8 * b + 4 + t, 1), :]
@@ -43,8 +50,7 @@
         last = grid[272:296, :] * table[tile, pl.ds(4 + t, 24, stride=8), :]
         last = last * table[tile, pl.ds(8 * 16 + t, 1), :]
         total = (acc[0:8] + acc[8:16]) + (last[0:8] + last[8:16] + last[16:24])
-        out.append(jnp.sum(total, axis=0, keepdims=True))
-    return jnp.concatenate(out, axis=0)
+        return jnp.sum(total, axis=0, keepdims=True)
 
 
 def fill(table, xy, rho_ref):
@@ -234,20 +240,33 @@
     loads[8].wait()
     box_copy.wait_recv()
 
-    def box_block(k, _):
+    def box_steps(k):
         lanes = pl.ds(pl.multiple_of(k * BLOCK, BLOCK), BLOCK)
         offset = cbox_ref[:, lanes] - b * BOXES
-        ids = lax.broadcasted_iota(jnp.int32, (BOXES, BLOCK), 0)
-        picked = jnp.dot(boxv[...], (ids == offset).astype(F32).astype(BF16), preferred_element_type=F32)
+        width = BOXES // PICKS
+        picked = None
+        for n in range(PICKS):
+            ids = lax.broadcasted_iota(jnp.int32, (width, BLOCK), 0) + n * width
+            term = jnp.dot(boxv[:, n * width:n * width + width], (ids == offset).astype(F32).astype(BF16), preferred_element_type=F32)
+            picked = term if picked is None else picked + term
+            yield
         ids = lax.broadcasted_iota(jnp.int32, (128, BLOCK), 0) + BOXES
         picked += jnp.dot(boxn[...], (ids == offset).astype(F32).astype(BF16), preferred_element_type=F32)
+        yield
         moved = jnp.dot(l2[...], picked.astype(BF16), preferred_element_type=F32)
+        yield
         for h in range(BLOCK // 128):
-            part = evaluate(moved[:, 128 * h:128 * h + 128], tscaled, k * (BLOCK // 128) + h)
-            potb[:, pl.ds(pl.multiple_of(k * BLOCK + 128 * h, 128), 128)] = part
-        return 0
-
-    lax.fori_loop(0, CTR // BLOCK, box_block, 0)
+            cols = pl.ds(pl.multiple_of(k * BLOCK + 128 * h, 128), 128)
+            for t in range(4):
+                potb[t:t + 1, cols] = evaluate_one(moved[:, 128 * h:128 * h + 128], tscaled, k * (BLOCK // 128) + h, t)
+                yield
+
+    def box_only(k, _):
+        for _ in box_steps(k):
+            pass
+        return 0
+
+    lax.fori_loop(0, BLOCKS // 2, box_only, 0)
 
     for _, share in margins:
         share.wait_recv()
@@ -262,39 +281,55 @@
     for copy in to_smem:
         copy.wait()
 
-    def gather(k, _):
-        c0 = k * UNROLL
-        lists = [idx_s.at[pl.ds(j * CTR + c0, UNROLL)] for j in range(7)]
-        for u in range(UNROLL):
+    def tail_steps(k):
+        near_round = acc[pl.ds(pl.multiple_of(k * BLOCK, BLOCK), BLOCK), :].astype(BF16)
+        direct = lax.dot_general(p2[...], near_round, (((1,), (1,)), ((), ())), preferred_element_type=F32)
+        yield
+        for h in range(BLOCK // 128):
+            cols = pl.ds(pl.multiple_of(k * BLOCK + 128 * h, 128), 128)
+            for t in range(4):
+                part = evaluate_one(direct[:, 128 * h:128 * h + 128], tplain, k * (BLOCK // 128) + h, t)
+                out_ref[t:t + 1, cols] = potb[t:t + 1, cols] + part
+                yield
+
+    def gather(k, add, steps):
+        c0 = k * BLOCK
+        lists = [idx_s.at[pl.ds(j * CTR + c0, BLOCK)] for j in range(7)]
+        for u in range(BLOCK):
+            if u % SPACING == 0:
+                next(steps, None)
             rows = [tab[pl.ds(lists[j][u], 1), :] for j in range(7)]
+            if add:
+                rows.append(acc[pl.ds(c0 + u, 1), :])
             while len(rows) > 1:
                 rows = [x + y for x, y in zip(rows[::2], rows[1::2])] + ([rows[-1]] if len(rows) % 2 else [])
             acc[pl.ds(c0 + u, 1), :] = rows[0]
-        return 0
-
-    lax.fori_loop(0, CTR // UNROLL, gather, 0)
+        for _ in steps:
+            pass
+
+    def early(k, _):
+        gather(k, False, box_steps(k + BLOCKS // 2))
+        return 0
+
+    def late(k, _):
+        gather(k, True, itertools.chain(tail_steps(k - BLOCKS // 2), tail_steps(k - 1)))
+        return 0
+
+    lax.fori_loop(0, BLOCKS // 2, early, 0)
 
     def take_far(o, _):
         answer(o).wait_recv()
         return 0
 
     lax.fori_loop(1, N_CTR, take_far, 0)
+    acc[pl.ds(CTR // 2, RING * FAR - CTR // 2), :] = jnp.zeros((RING * FAR - CTR // 2, SRC), F32)
     for m in range(RING):
         rows = far[lax.rem(m + r, RING)].astype(F32)
         at = pl.ds(m, FAR, stride=RING)
         acc[at, :] = acc[at, :] + rows
-
-    def near_block(k, _):
-        lanes = pl.ds(pl.multiple_of(k * BLOCK, BLOCK), BLOCK)
-        near_round = acc[lanes, :].astype(BF16)
-        direct = lax.dot_general(p2[...], near_round, (((1,), (1,)), ((), ())), preferred_element_type=F32)
-        for h in range(BLOCK // 128):
-            part = evaluate(direct[:, 128 * h:128 * h + 128], tplain, k * (BLOCK // 128) + h)
-            cols = pl.ds(pl.multiple_of(k * BLOCK + 128 * h, 128), 128)
-            out_ref[:, cols] = potb[:, cols] + part
-        return 0
-
-    lax.fori_loop(0, CTR // BLOCK, near_block, 0)
+    lax.fori_loop(BLOCKS // 2, BLOCKS, late, 0)
+    for _ in tail_steps(BLOCKS - 1):
+        pass
 
     box_copy.wait_send()
     for group in margins:

time: 36.4 us -> 32.6 us (0.90)
  Pallas kernels: 34.8 us -> 31 us
    pallas_call x1, Pallas kernels: 34.8 us -> 31 us  [shards(): pl.pallas_call(kernel, out_shape=jax.ShapeDtypeStruct((4, CTR), F32), in_...]
where the time goes in v3:
time: 32.6 us; the launch traced here: 32.4 us
  Pallas kernels  31 us (95%)
  local copies, waits for them, and re-layouts  1.38 us (4%)
    pallas_call x1, Pallas kernels, shards(): pl.pallas_call(kernel, out_shape=jax.ShapeDtypeStruct((4, CTR), F32), in_...  31 us
    unnamed x1, local copies, waits for them, and re-layouts  1.38 us

profile of v3, /device:TPU:0, one launch (start us, length us, event | category | flops | bytes accessed | tf_op | source)
XLA Modules:
  0.0 32.4 jit_solution(603711954763789084)
XLA Ops:
  0.0 31.0 %qbx.1 = f32[4,2048]{1,0:T(4,128)} custom-call(bf16[289,2048]{1,0:T(8,128)(2,1)} %box_hbm.1, s32[1,2048]{1,0:T(1,128)} %bitcast.3, f32[1,2048]{1,0:T(1,128)} %bitcast.4, bf16[8192,128]{1,0:T(8,128)(2,1)} %pan_hbm.1, s32[8,2048]{1,0:T(8,128)} %near_hbm.1, s32[1,2048]{1,0:T(1,128)} %bitcast.5, bf16[289,289]{1,0:T(8,128)(2,1)} %l2l_hbm.1, ...), custom_call_target="tpu_custom_call" | custom-call | tf_op jit(solution)/shard_map/qbx/pallas_call | solution.py:351
  31.0 1.4 %copy.11 = f32[4,2048]{1,0:T(4,128)} copy(f32[4,2048]{1,0:T(4,128)} %qbx.1) | data formatting | bytes 65536

commit v4 on v3

--- a/solution.py
+++ b/solution.py
@@ -30,6 +30,8 @@
 BLOCK = 256
 BLOCKS = CTR // BLOCK
 PICKS = 4
+AHEAD = 1
+FIRST = 5
 SPACING = 14
 MESH = pl.DeviceIdType.MESH
 F32 = jnp.float32
@@ -41,37 +43,40 @@
 
 
 def evaluate_one(grid, table, tile, t):
-    if True:
-        acc = None
-        for b in range(DEG):
-            term = grid[16 * b:16 * b + 16, :] * table[tile, pl.ds(8 * b + 4 + t, 1), :]
-            acc = term if acc is None else acc + term
-        acc = acc * table[tile, pl.ds(t, 16, stride=8), :]
-        last = grid[272:296, :] * table[tile, pl.ds(4 + t, 24, stride=8), :]
-        last = last * table[tile, pl.ds(8 * 16 + t, 1), :]
-        total = (acc[0:8] + acc[8:16]) + (last[0:8] + last[8:16] + last[16:24])
-        return jnp.sum(total, axis=0, keepdims=True)
+    acc = None
+    for b in range(DEG):
+        term = grid[16 * b:16 * b + 16, :] * table[tile, pl.ds(8 * b + 4 + t, 1), :]
+        acc = term if acc is None else acc + term
+    acc = acc * table[tile, pl.ds(t, 16, stride=8), :]
+    last = grid[272:296, :] * table[tile, pl.ds(4 + t, 24, stride=8), :]
+    last = last * table[tile, pl.ds(8 * 16 + t, 1), :]
+    total = (acc[0:8] + acc[8:16]) + (last[0:8] + last[8:16] + last[16:24])
+    return jnp.sum(total, axis=0, keepdims=True)
 
 
 def fill(table, xy, rho_ref):
     def one(tile, _):
-        lanes = pl.ds(pl.multiple_of(tile * 128, 128), 128)
-        x = jnp.concatenate([xy[0, :, lanes], xy[1, :, lanes]], axis=0)
-        square = None
-        if rho_ref is not None:
-            rho = rho_ref[:, lanes]
-            x, square = x * rho, rho * rho
-        before, now = jnp.ones_like(x), x
-        table[tile, pl.ds(0, 8), :] = before
-        table[tile, pl.ds(8, 8), :] = now
-        for n in range(2, DEG):
-            later = 2.0 * x * now - (before if square is None else square * before)
-            table[tile, pl.ds(8 * n, 8), :] = later
-            before, now = now, later
-        table[tile, pl.ds(8 * DEG, 56), :] = jnp.zeros((56, 128), F32)
+        fill_tile(table, xy, rho_ref, tile)
         return 0
 
     lax.fori_loop(0, CTR // 128, one, 0)
+
+
+def fill_tile(table, xy, rho_ref, tile):
+    lanes = pl.ds(pl.multiple_of(tile * 128, 128), 128)
+    x = jnp.concatenate([xy[0, :, lanes], xy[1, :, lanes]], axis=0)
+    square = None
+    if rho_ref is not None:
+        rho = rho_ref[:, lanes]
+        x, square = x * rho, rho * rho
+    before, now = jnp.ones_like(x), x
+    table[tile, pl.ds(0, 8), :] = before
+    table[tile, pl.ds(8, 8), :] = now
+    for n in range(2, DEG):
+        later = 2.0 * x * now - (before if square is None else square * before)
+        table[tile, pl.ds(8 * n, 8), :] = later
+        before, now = now, later
+    table[tile, pl.ds(8 * DEG, 56), :] = jnp.zeros((56, 128), F32)
 
 
 def kernel(
@@ -178,7 +183,6 @@
     lax.fori_loop(0, PAN // 512, widen, 0)
     loads[3].wait()
     loads[4].wait()
-    fill(tplain, xy_ref, None)
     fill(tscaled, xy_ref, rho_ref)
     loads[5].wait()
     loads[6].wait()
@@ -230,10 +234,7 @@
     lax.fori_loop(0, 12, serve, 0)
     lax.fori_loop(1, 4, serve_column, 0)
 
-    for fetch, share in margins:
-        fetch.wait_recv()
-        share.start()
-    for o in FAR_ORDER:
+    for o in FAR_ORDER[:FIRST]:
         answer(o).start()
 
     loads[7].wait()
@@ -266,7 +267,13 @@
             pass
         return 0
 
-    lax.fori_loop(0, BLOCKS // 2, box_only, 0)
+    lax.fori_loop(0, AHEAD, box_only, 0)
+    for fetch, share in margins:
+        fetch.wait_recv()
+        share.start()
+    for o in FAR_ORDER[FIRST:]:
+        answer(o).start()
+    lax.fori_loop(AHEAD, BLOCKS // 2, box_only, 0)
 
     for _, share in margins:
         share.wait_recv()
@@ -307,8 +314,14 @@
         for _ in steps:
             pass
 
+    def plain_steps(k):
+        tiles = CTR // 128 // (BLOCKS // 2)
+        for n in range(tiles):
+            fill_tile(tplain, xy_ref, None, k * tiles + n)
+            yield
+
     def early(k, _):
-        gather(k, False, box_steps(k + BLOCKS // 2))
+        gather(k, False, itertools.chain(box_steps(k + BLOCKS // 2), plain_steps(k)))
         return 0
 
     def late(k, _):

time: 32.6 us -> 31.7 us (0.972)
  Pallas kernels: 31 us -> 30.1 us
    pallas_call x1, Pallas kernels: 31 us -> 30.1 us  [shards(): pl.pallas_call(kernel, out_shape=jax.ShapeDtypeStruct((4, CTR), F32), in_...]
where the time goes in v4:
time: 31.7 us; the launch traced here: 31.5 us
  Pallas kernels  30.1 us (95%)
  local copies, waits for them, and re-layouts  1.38 us (4%)
    pallas_call x1, Pallas kernels, shards(): pl.pallas_call(kernel, out_shape=jax.ShapeDtypeStruct((4, CTR), F32), in_...  30.1 us
    unnamed x1, local copies, waits for them, and re-layouts  1.38 us

profile of v4, /device:TPU:0, one launch (start us, length us, event | category | flops | bytes accessed | tf_op | source)
XLA Modules:
  0.0 31.5 jit_solution(17665676713040012441)
XLA Ops:
  0.0 30.1 %qbx.1 = f32[4,2048]{1,0:T(4,128)} custom-call(bf16[289,2048]{1,0:T(8,128)(2,1)} %box_hbm.1, s32[1,2048]{1,0:T(1,128)} %bitcast.3, f32[1,2048]{1,0:T(1,128)} %bitcast.4, bf16[8192,128]{1,0:T(8,128)(2,1)} %pan_hbm.1, s32[8,2048]{1,0:T(8,128)} %near_hbm.1, s32[1,2048]{1,0:T(1,128)} %bitcast.5, bf16[289,289]{1,0:T(8,128)(2,1)} %l2l_hbm.1, ...), custom_call_target="tpu_custom_call" | custom-call | tf_op jit(solution)/shard_map/qbx/pallas_call | solution.py:364
  30.1 1.4 %copy.11 = f32[4,2048]{1,0:T(4,128)} copy(f32[4,2048]{1,0:T(4,128)} %qbx.1) | data formatting | bytes 65536

commit v5 on v4

--- a/solution.py
+++ b/solution.py
@@ -31,7 +31,7 @@
 BLOCKS = CTR // BLOCK
 PICKS = 4
 AHEAD = 1
-FIRST = 5
+FIRST = 8
 SPACING = 14
 MESH = pl.DeviceIdType.MESH
 F32 = jnp.float32

time: 31.7 us -> 31.7 us (level)
  no operation moved by 1% of the time
where the time goes in v5:
time: 31.7 us; the launch traced here: 31.5 us
  Pallas kernels  30.1 us (95%)
  local copies, waits for them, and re-layouts  1.38 us (4%)
    pallas_call x1, Pallas kernels, shards(): pl.pallas_call(kernel, out_shape=jax.ShapeDtypeStruct((4, CTR), F32), in_...  30.1 us
    unnamed x1, local copies, waits for them, and re-layouts  1.38 us

profile of v5, /device:TPU:0, one launch (start us, length us, event | category | flops | bytes accessed | tf_op | source)
XLA Modules:
  0.0 31.5 jit_solution(4318569161909043188)
XLA Ops:
  0.0 30.1 %qbx.1 = f32[4,2048]{1,0:T(4,128)} custom-call(bf16[289,2048]{1,0:T(8,128)(2,1)} %box_hbm.1, s32[1,2048]{1,0:T(1,128)} %bitcast.3, f32[1,2048]{1,0:T(1,128)} %bitcast.4, bf16[8192,128]{1,0:T(8,128)(2,1)} %pan_hbm.1, s32[8,2048]{1,0:T(8,128)} %near_hbm.1, s32[1,2048]{1,0:T(1,128)} %bitcast.5, bf16[289,289]{1,0:T(8,128)(2,1)} %l2l_hbm.1, ...), custom_call_target="tpu_custom_call" | custom-call | tf_op jit(solution)/shard_map/qbx/pallas_call | solution.py:364
  30.1 1.4 %copy.11 = f32[4,2048]{1,0:T(4,128)} copy(f32[4,2048]{1,0:T(4,128)} %qbx.1) | data formatting | bytes 65536
